TPU v7x, 256 devices: a whole 4x4x8 slice. The times are simulated.
256 devices in a mesh: tower: 8 (over x, core), peer: 32 (over z, y).
Axes of the slice: x: 4, y: 4, z: 8, core: 2. Of those that a mesh axis runs over, the one named last changes fastest.
Arguments:
- embeddings: bfloat16 [16384, 2048], P('tower', 'peer'), may hold values from -6 to 6
- session_lists: int32 [8, 2048], P('tower'), may hold values from 0 to 2047, each once within a row
- owners: int32 [16384, 1], P(('tower', 'peer')), may hold values from 0 to 7; in each aligned block of 64 rows (0 to 63, 64 to 127, ...) at most 16 rows name the same one
- counts: int32 [16384], P(('tower', 'peer')), may hold values from 1 to 3, as said below
- item_feats: bfloat16 [98304, 256], P(('tower', 'peer')), may hold values from -6 to 6
- cotangent: bfloat16 [98304, 1024], P(('tower', 'peer')), may hold values from -6 to 6
- cross_down: bfloat16 [2048, 256], replicated, may hold values from -0.125 to 0.125
- cross_up: bfloat16 [256, 2048], replicated, may hold values from -0.375 to 0.375
- compress: bfloat16 [2048, 256], replicated, may hold values from -0.125 to 0.125
- over_first: bfloat16 [512, 4096], replicated, may hold values from -0.25 to 0.25
- over_second: bfloat16 [4096, 1024], P('peer'), may hold values from -0.09375 to 0.09375
- over_third: bfloat16 [1024, 1024], replicated, may hold values from -0.1875 to 0.1875
Outputs:
- over_out: bfloat16 [98304, 1024], P(('tower', 'peer'))
- emb_grad: bfloat16 [16384, 2048], P('tower', 'peer')
Inputs may be any that keep to these rules, and one draw needn't show every extreme that they name: `session_lists`: each row is a permutation of the tower's 64 * 32 table rows. `owners`: within the 64 sessions of one device, no tower owns more than 16 of them. `counts`: the first session of every device has 3 samples and the second has one.
All inputs are finite; a program needn't handle non-finite values.
Results may differ from a plain program's by a relative error of at most 0.02.
Values may be sent and summed in bfloat16 or wider, within the bound.
A program may use at most 128 MiB of HBM per device.

v0:
```python
import jax
import jax.numpy as jnp
from jax import lax
from jax.sharding import PartitionSpec as P

MOSTC = 3


def silu_slope(pre):
    sigma = jax.nn.sigmoid(pre)
    return sigma * (1.0 + pre * (1.0 - sigma))


def times_t(left, right):
    return lax.dot_general(
        left, right, (((1,), (1,)), ((), ())), preferred_element_type=jnp.float32
    )


def body(
    embeddings,
    session_lists,
    owners,
    counts,
    item_feats,
    cotangent,
    cross_down,
    cross_up,
    compress,
    over_first,
    over_second,
    over_third,
):
    towers = lax.axis_size("tower")
    comp_width = compress.shape[1]
    grid_rows = item_feats.shape[0]
    slots = grid_rows // (towers * MOSTC)
    order = session_lists[0]
    picked = jnp.take(embeddings, order, axis=0)
    session_rows = lax.all_to_all(picked, "peer", split_axis=0, concat_axis=1, tiled=True)
    low = jnp.dot(session_rows, cross_down, preferred_element_type=jnp.float32).astype(jnp.bfloat16)
    lift = jnp.dot(low, cross_up, preferred_element_type=jnp.float32)
    rows_wide = session_rows.astype(jnp.float32)
    crossed = (rows_wide * lift + rows_wide).astype(jnp.bfloat16)
    compressed = jnp.dot(crossed, compress, preferred_element_type=jnp.float32).astype(jnp.bfloat16)
    owner_list = owners[:, 0]
    choose = (owner_list[:, None] == jnp.arange(towers, dtype=jnp.int32)[None, :]).astype(jnp.int32)
    earlier = jnp.cumsum(choose, axis=0) - choose
    position = jnp.sum(choose * earlier, axis=1)
    target = owner_list * slots + position
    dispatch = (target[:, None] == jnp.arange(towers * slots, dtype=jnp.int32)[None, :]).astype(
        jnp.int32
    )
    dispatch_half = dispatch.astype(jnp.bfloat16)
    send_rows = lax.dot_general(
        dispatch_half, compressed, (((0,), (0,)), ((), ())), preferred_element_type=jnp.float32
    ).astype(jnp.bfloat16)
    send_counts = jnp.sum(dispatch * counts[:, None], axis=0)
    repeated = jnp.broadcast_to(send_rows[:, None, :], (towers * slots, MOSTC, comp_width))
    repeated = repeated.reshape(towers, slots * MOSTC, comp_width)
    got_rows, got_counts = (
        lax.all_to_all(repeated, "tower", split_axis=0, concat_axis=0, tiled=True),
        lax.all_to_all(
            send_counts.reshape(towers, slots), "tower", split_axis=0, concat_axis=0, tiled=True
        ),
    )
    expanded = got_rows.reshape(grid_rows, comp_width)
    live = (
        jnp.arange(MOSTC, dtype=jnp.int32)[None, :] < got_counts.reshape(towers * slots)[:, None]
    ).astype(jnp.float32)
    live = live.reshape(grid_rows)
    inputs = jnp.concatenate([expanded, item_feats], axis=1)
    pre_first = jnp.dot(inputs, over_first, preferred_element_type=jnp.float32)
    hidden_first = jax.nn.silu(pre_first).astype(jnp.bfloat16)
    pre_second = jnp.dot(
        hidden_first,
        lax.all_gather(over_second, "peer", axis=0, tiled=True),
        preferred_element_type=jnp.float32,
    )
    hidden_second = jax.nn.silu(pre_second).astype(jnp.bfloat16)
    over_out = (
        jnp.dot(hidden_second, over_third, preferred_element_type=jnp.float32) * live[:, None]
    ).astype(jnp.bfloat16)
    masked = cotangent * live[:, None].astype(jnp.bfloat16)
    grad_second = (times_t(masked, over_third) * silu_slope(pre_second)).astype(jnp.bfloat16)
    back_first = times_t(grad_second, lax.all_gather(over_second, "peer", axis=0, tiled=True))
    grad_first = (back_first * silu_slope(pre_first)).astype(jnp.bfloat16)
    sample_grad = times_t(grad_first, over_first[:comp_width]).astype(jnp.bfloat16)
    returned = lax.all_to_all(
        sample_grad.reshape(towers, slots * MOSTC, comp_width),
        "tower",
        split_axis=0,
        concat_axis=0,
        tiled=True,
    )
    slot_grad = jnp.sum(
        returned.astype(jnp.float32).reshape(towers * slots, MOSTC, comp_width), axis=1
    ).astype(jnp.bfloat16)
    session_grad = jnp.dot(dispatch_half, slot_grad, preferred_element_type=jnp.float32).astype(
        jnp.bfloat16
    )
    grad_crossed = times_t(session_grad, compress).astype(jnp.bfloat16)
    grad_lift = (grad_crossed.astype(jnp.float32) * rows_wide).astype(jnp.bfloat16)
    grad_low = times_t(grad_lift, cross_up).astype(jnp.bfloat16)
    grad_rows = (
        grad_crossed.astype(jnp.float32) * (lift + 1.0) + times_t(grad_low, cross_down)
    ).astype(jnp.bfloat16)
    columns_back = lax.all_to_all(grad_rows, "peer", split_axis=1, concat_axis=0, tiled=True)
    emb_grad = jnp.zeros_like(embeddings).at[order].set(columns_back)
    return (over_out, emb_grad)


def solution(mesh):
    return jax.shard_map(
        body,
        mesh=mesh,
        in_specs=(
            P("tower", "peer"),
            P("tower", None),
            P(("tower", "peer"), None),
            P(("tower", "peer")),
            P(("tower", "peer"), None),
            P(("tower", "peer"), None),
            P(),
            P(),
            P(),
            P(),
            P("peer", None),
            P(),
        ),
        out_specs=(P(("tower", "peer"), None), P("tower", "peer")),
        check_vma=False,
    )
```

profile of v0, /device:TPU:1, one launch (start us, length us, event | category | flops | bytes accessed | tf_op | source)
XLA Modules:
  0.0 186.6 jit_solution(9144501375350728294)
XLA Ops:
  7.2 0.0 copy-start
  7.2 0.0 all-gather.2.cloned.1.call-start
  7.2 0.7 all-gather.2.cloned.1.call-update
  7.9 0.7 fusion.25
  8.6 0.1 reduce_window_sum.11
  8.7 0.8 select_reduce_fusion.1
  9.6 0.7 fusion.29
  10.2 0.7 select_reduce_fusion
  11.0 0.7 all_to_all.42
  11.7 6.5 %all-to-all-start.2 = ((s32[8,1,16]{2,1,0:T(1,128)}), s32[8,1,16]{2,1,0:T(1,128)S(1)}, u32[]{:S(2)}, u32[]{:S(2)}) async-start(s32[8,1,16]{2,1,0:T(1,128)} %bitcast.8), calls=%async_computation.2 | async-start | bytes 8192 | tf_op jit(solution)/shard_map/all_to_all | solution.py:63
  18.1 1.2 copy.28
  19.4 0.5 broadcast.66
  19.8 1.3 reduce.7
  21.1 0.1 squeeze.6
  21.2 0.7 compare_select_fusion
  21.9 6.2 %gather_fusion = bf16[2048,64]{1,0:T(8,128)(2,1)S(1)} fusion(bf16[2048,64]{1,0:T(8,128)(2,1)S(1)} %copy.28, s32[2048]{0:T(1024)S(1)} %broadcast_clamp_fusion), kind=kCustom, calls=%fused_computation | custom fusion | bytes 532480 | tf_op jit(solution)/shard_map/jit(_take)/gather | solution.py:39
  28.1 0.3 broadcast_select_fusion
  28.5 1.1 reshape.142
  29.6 0.0 all-to-all-done.2
  29.6 10.6 %all-to-all-start = ((bf16[32,2,2048]{2,1,0:T(2,128)(2,1)}), bf16[32,2,2048]{2,1,0:T(2,128)(2,1)S(1)}, u32[]{:S(2)}, u32[]{:S(2)}) async-start(bf16[32,2,2048]{2,1,0:T(2,128)(2,1)} %reshape.142), calls=%async_computation | async-start | bytes 524288 | tf_op jit(solution)/shard_map/all_to_all | solution.py:40
  40.2 0.6 reduce.8
  40.7 0.1 lt.53
  40.8 13.4 %all-to-all-done = bf16[32,2,2048]{2,1,0:T(2,128)(2,1)S(1)} async-done(((bf16[32,2,2048]{2,1,0:T(2,128)(2,1)}), bf16[32,2,2048]{2,1,0:T(2,128)(2,1)S(1)}, u32[]{:S(2)}, u32[]{:S(2)}) %all-to-all-start) | async-done | bytes 262176 | tf_op jit(solution)/shard_map/all_to_all | solution.py:40
  54.2 0.4 reshape.143
  54.5 0.3 copy.29
  54.9 0.5 all_to_all.40
  55.4 0.0 copy-start.1
  55.4 2.4 %fusion.8 = f32[64,2048]{1,0:T(8,128)S(1)} fusion(bf16[256,2048]{1,0:T(8,128)(2,1)} %param.19, bf16[64,2048]{1,0:T(8,128)(2,1)S(1)} %all_to_all.40, bf16[2048,256]{1,0:T(8,128)(2,1)} %param.18), kind=kOutput, calls=%fused_computation.22 | convolution fusion | flops 134234112 | bytes 2883584 | tf_op jit(solution)/shard_map/dot_general | solution.py:42
  57.7 1.7 convolution_convert_fusion.1
  59.4 0.1 broadcast_in_dim.16
  59.5 0.8 reshape.102
  60.4 5.8 %all-to-all-start.1 = ((bf16[8,48,256]{2,1,0:T(8,128)(2,1)}), bf16[8,48,256]{2,1,0:T(8,128)(2,1)S(1)}, u32[]{:S(2)}, u32[]{:S(2)}) async-start(bf16[8,48,256]{2,1,0:T(8,128)(2,1)} %reshape.102), calls=%async_computation.1 | async-start | bytes 393216 | tf_op jit(solution)/shard_map/all_to_all | solution.py:62
  66.2 0.1 fusion.24
  66.3 0.2 reshape.107
  66.5 5.6 %all-to-all-done.1 = bf16[8,48,256]{2,1,0:T(8,128)(2,1)S(1)} async-done(((bf16[8,48,256]{2,1,0:T(8,128)(2,1)}), bf16[8,48,256]{2,1,0:T(8,128)(2,1)S(1)}, u32[]{:S(2)}, u32[]{:S(2)}) %all-to-all-start.1) | async-done | bytes 196640 | tf_op jit(solution)/shard_map/all_to_all | solution.py:62
  72.1 0.0 copy-done.1
  72.1 6.7 %fusion.13 = f32[384,4096]{1,0:T(8,128)} fusion(bf16[512,4096]{1,0:T(8,128)(2,1)} %param.21, bf16[384,256]{1,0:T(8,128)(2,1)S(1)} %copy-done.1, bf16[384,256]{1,0:T(8,128)(2,1)S(1)} %bitcast.39), kind=kOutput, calls=%fused_computation.30 | convolution fusion | flops 1611399168 | bytes 10878976 | tf_op jit(solution)/shard_map/dot_general | solution.py:73
  78.8 36.3 %all-gather.2.cloned.1.call-done = bf16[4096,1024]{1,0:T(8,128)(2,1)} async-done(((bf16[128,1024]{1,0:T(8,128)(2,1)}), bf16[4096,1024]{1,0:T(8,128)(2,1)}) %all-gather.2.cloned.1.call-update) | async-done | bytes 8388624 | tf_op jit(solution)/shard_map/all_gather | solution.py:77
  115.1 0.0 copy-start.2
  115.1 8.1 %fusion = f32[384,1024]{1,0:T(8,128)S(1)} fusion(bf16[4096,1024]{1,0:T(8,128)(2,1)} %all-gather.2.cloned.1.call-done, f32[384,4096]{1,0:T(8,128)} %fusion.13), kind=kOutput, calls=%fused_computation.5 | convolution fusion | flops 3229089792 | bytes 16252928 | tf_op jit(solution)/shard_map/dot_general | solution.py:75
  123.2 0.0 copy-start.3
  123.2 1.2 copy-done.3
  124.4 0.0 copy-done
  124.4 0.0 copy-done.2
  124.4 2.1 %multiply_convert_fusion.3 = bf16[384,1024]{1,0:T(8,128)(2,1)} fusion(f32[384,1024]{1,0:T(8,128)S(1)} %fusion, bf16[1024,1024]{1,0:T(8,128)(2,1)S(1)} %copy-done, bf16[384,1024]{1,0:T(8,128)(2,1)S(1)} %copy-done.2, bf16[384]{0:T(512)(128)(2,1)S(1)} %convert_element_type.100), kind=kOutput, calls=%fused_computation.12 | convolution fusion | flops 809238528 | bytes 5243648 | tf_op jit(solution)/shard_map/dot_general | solution.py:15
  126.5 10.5 %fusion.5 = bf16[384,256]{1,0:T(8,128)(2,1)S(1)} fusion(bf16[512,4096]{1,0:T(8,128)(2,1)} %param.21, f32[384,4096]{1,0:T(8,128)} %fusion.13, bf16[384,1024]{1,0:T(8,128)(2,1)} %multiply_convert_fusion.3, bf16[4096,1024]{1,0:T(8,128)(2,1)} %all-gather.2.cloned.1.call-done), kind=kOutput, calls=%fused_computation.16 | convolution fusion | flops 4040785920 | bytes 17760256 | tf_op jit(solution)/shard_map/dot_general | solution.py:15
  137.1 11.0 %all_to_all.54 = bf16[8,48,256]{2,1,0:T(8,128)(2,1)S(1)} all-to-all(bf16[8,48,256]{2,1,0:T(8,128)(2,1)S(1)} %bitcast.41), channel_id=1, replica_groups=mesh['tower'=8,'peer'=32] {'tower'}, dimensions={0} | all-to-all | bytes 393216 | tf_op jit(solution)/shard_map/all_to_all | solution.py:89
  148.1 0.1 reshape.105
  148.2 0.3 reduce
  148.5 1.8 fusion.2
  150.3 3.5 %fusion.1 = bf16[64,2048]{1,0:T(8,128)(2,1)} fusion(bf16[2048,256]{1,0:T(8,128)(2,1)} %param.18, bf16[256,2048]{1,0:T(8,128)(2,1)} %param.19, f32[64,2048]{1,0:T(8,128)S(1)} %fusion.2, f32[64,2048]{1,0:T(8,128)S(1)} %fusion.8, bf16[64,2048]{1,0:T(8,128)(2,1)S(1)} %all_to_all.40), kind=kOutput, calls=%fused_computation.7 | convolution fusion | flops 135151616 | bytes 3670016 | tf_op jit(solution)/shard_map/dot_general | solution.py:15
  153.8 1.5 all_to_all.45
  155.3 0.2 copy.34
  155.5 1.1 reshape.144
  156.6 5.6 %all-to-all-start.4 = ((bf16[32,2,2048]{2,1,0:T(2,128)(2,1)}), bf16[32,2,2048]{2,1,0:T(2,128)(2,1)S(1)}, u32[]{:S(2)}, u32[]{:S(2)}) async-start(bf16[32,2,2048]{2,1,0:T(2,128)(2,1)} %reshape.144), calls=%async_computation.4 | async-start | bytes 524288 | tf_op jit(solution)/shard_map/all_to_all | solution.py:108
  162.2 3.3 %multiply_convert_fusion.4 = bf16[384,1024]{1,0:T(8,128)(2,1)} fusion(bf16[1024,1024]{1,0:T(8,128)(2,1)S(1)} %copy-done, f32[384,1024]{1,0:T(8,128)} %copy-done.3, f32[384]{0:T(512)S(1)} %reshape.107), kind=kOutput, calls=%fused_computation.13 | convolution fusion | flops 808058880 | bytes 4457984 | tf_op jit(solution)/shard_map/dot_general | solution.py:82
  165.5 7.2 %all-to-all-done.4 = bf16[32,2,2048]{2,1,0:T(2,128)(2,1)S(1)} async-done(((bf16[32,2,2048]{2,1,0:T(2,128)(2,1)}), bf16[32,2,2048]{2,1,0:T(2,128)(2,1)S(1)}, u32[]{:S(2)}, u32[]{:S(2)}) %all-to-all-start.4) | async-done | bytes 262176 | tf_op jit(solution)/shard_map/all_to_all | solution.py:108
  172.6 0.4 reshape.145
  173.0 5.9 %scatter_custom_fusion = bf16[2048,64]{1,0:T(8,128)(2,1)S(1)} fusion(s32[2048]{0:T(1024)S(1)} %bitcast.43, bf16[2048,64]{1,0:T(8,128)(2,1)S(1)} %bitcast.40, bf16[]{:T(256)} %constant.36.clone.1), kind=kCustom, calls=%fused_computation.35 | custom fusion | bytes 262146 | tf_op jit(solution)/shard_map/scatter | solution.py:109
  178.9 0.9 copy.32
  (3 shorter events, 0.0 us)
Async XLA Ops:
  7.2 117.2 %copy-start = (bf16[1024,1024]{1,0:T(8,128)(2,1)S(1)}, bf16[1024,1024]{1,0:T(8,128)(2,1)}, u32[]{:S(2)}) copy-start(bf16[1024,1024]{1,0:T(8,128)(2,1)} %param.23) | copy-start | bytes 6291460
  7.2 107.9 %all-gather.2.cloned.1.call-start = ((), (), s32[]{:S(2)}) async-start(), calls=%async_computation.5 | async-start | bytes 8650752 | tf_op jit(solution)/shard_map/all_gather | solution.py:77
  11.7 17.9 %all-to-all-start.2 = ((s32[8,1,16]{2,1,0:T(1,128)}), s32[8,1,16]{2,1,0:T(1,128)S(1)}, u32[]{:S(2)}, u32[]{:S(2)}) async-start(s32[8,1,16]{2,1,0:T(1,128)} %bitcast.8), calls=%async_computation.2 | async-start | bytes 8192 | tf_op jit(solution)/shard_map/all_to_all | solution.py:63
  29.6 24.6 %all-to-all-start = ((bf16[32,2,2048]{2,1,0:T(2,128)(2,1)}), bf16[32,2,2048]{2,1,0:T(2,128)(2,1)S(1)}, u32[]{:S(2)}, u32[]{:S(2)}) async-start(bf16[32,2,2048]{2,1,0:T(2,128)(2,1)} %reshape.142), calls=%async_computation | async-start | bytes 524288 | tf_op jit(solution)/shard_map/all_to_all | solution.py:40
  55.4 16.8 %copy-start.1 = (bf16[384,256]{1,0:T(8,128)(2,1)S(1)}, bf16[384,256]{1,0:T(8,128)(2,1)}, u32[]{:S(2)}) copy-start(bf16[384,256]{1,0:T(8,128)(2,1)} %param.16) | copy-start | bytes 589828
  60.4 11.7 %all-to-all-start.1 = ((bf16[8,48,256]{2,1,0:T(8,128)(2,1)}), bf16[8,48,256]{2,1,0:T(8,128)(2,1)S(1)}, u32[]{:S(2)}, u32[]{:S(2)}) async-start(bf16[8,48,256]{2,1,0:T(8,128)(2,1)} %reshape.102), calls=%async_computation.1 | async-start | bytes 393216 | tf_op jit(solution)/shard_map/all_to_all | solution.py:62
  115.1 9.3 %copy-start.2 = (bf16[384,1024]{1,0:T(8,128)(2,1)S(1)}, bf16[384,1024]{1,0:T(8,128)(2,1)}, u32[]{:S(2)}) copy-start(bf16[384,1024]{1,0:T(8,128)(2,1)} %param.17) | copy-start | bytes 2359300
  123.2 1.2 copy-start.3
  156.6 16.0 %all-to-all-start.4 = ((bf16[32,2,2048]{2,1,0:T(2,128)(2,1)}), bf16[32,2,2048]{2,1,0:T(2,128)(2,1)S(1)}, u32[]{:S(2)}, u32[]{:S(2)}) async-start(bf16[32,2,2048]{2,1,0:T(2,128)(2,1)} %reshape.144), calls=%async_computation.4 | async-start | bytes 524288 | tf_op jit(solution)/shard_map/all_to_all | solution.py:108
Sparse Core Ops, SparseCore 0:
  10.6 104.4 all-gather.1
where the time goes:
time: 188 us; the launch traced here: 187 us
  waiting for transfers between devices  63.1 us (34%)
  matrix products  40.1 us (21%)
  starting transfers between devices  28.4 us (15%)
  local copies, waits for them, and re-layouts  23.3 us (12%)
  between operations  14.2 us (8%)
  blocking collectives  11 us (6%)
  other arithmetic  6.42 us (3%)
    all_gather x1, waiting for transfers between devices, body(): lax.all_gather(over_second, 'peer', axis=0, tiled=True)  36.3 us
    dot_general x4, matrix products, times_t(): lax.dot_general(left, right, (((1,), (1,)), ((), ())), preferred_element_...  18 us
    all_to_all x1, waiting for transfers between devices, body(): lax.all_to_all(picked, 'peer', split_axis=0, concat_axis=1, tiled=True)  13.4 us
    all_to_all x1, blocking collectives, body(): lax.all_to_all(sample_grad.reshape(towers, slots * MOSTC, comp_width), 't...  11 us
    all_to_all x1, starting transfers between devices, body(): lax.all_to_all(picked, 'peer', split_axis=0, concat_axis=1, tiled=True)  10.6 us
    dot_general x1, matrix products, body(): jnp.dot(hidden_first, lax.all_gather(over_second, 'peer', axis=0, tiled=T...  8.11 us
    all_to_all x1, waiting for transfers between devices, body(): lax.all_to_all(grad_rows, 'peer', split_axis=1, concat_axis=0, tiled=True)  7.16 us
    unnamed x15, local copies, waits for them, and re-layouts  6.71 us
  transfers between devices with their start and end apart: 5, of which 4 were waited for; matrix products, arithmetic and copies ran while one was open for 17% of the time, Pallas kernels for 0%

commit v1 on v0

v1 whole, which is shorter than its diff:
```python
import jax
import jax.numpy as jnp
from jax import lax
from jax.experimental import pallas as pl
from jax.experimental.pallas import tpu as pltpu
from jax.sharding import PartitionSpec as P

MESH = pl.DeviceIdType.MESH
F32 = jnp.float32
BF16 = jnp.bfloat16
NX, NC, NY, NZ = 4, 2, 4, 8
NP, NT = NY * NZ, NX * NC
ROWS, SLOTS, MOSTC, CAP = 384, 128, 3, 16
UDEV = 64
FEAT, WIDE = 2048, 256
H1, H2 = 4096, 1024
HZ = H1 // NZ
HS = H1 // NP
LISTED = UDEV * NP
FOLD = 4
RBLK = LISTED // FOLD
ZREL = (0, 7, 1, 6, 2, 5, 3, 4)
BATCH = ((0, 1), (1, 2), (3, 2), (5, 3))


def dot(a, b):
    return jnp.dot(a, b, preferred_element_type=F32)


def dot_t(a, b):
    return lax.dot_general(a, b, (((1,), (1,)), ((), ())), preferred_element_type=F32)


def wrap(v, n):
    return lax.rem(v + 2 * n, n)


def iota(shape, axis):
    return lax.broadcasted_iota(jnp.int32, shape, axis)


def kernel(
    emb, lists, owners, counts, item, cot, cd, cu, comp, of, w2, ot,
    out_hbm, eg_hbm,
    embv, listv, ownv, cntv, itemv, cotv, cdv, cuv, compv, ofv, W2, otv,
    hot, pay, arr, SR, lift, tsend, trecv, gsend, grecv, bpay, barr, egv,
    prei, hid, slope, pre2, g3, hs, gs2, outv, sacc,
    lsem, asend, arecv, tsem, trsem, gsem, grsem, bsend, brecv,
    zs, zr, ys, yr, xs, xr, ds, dr,
):
    t = lax.axis_index("tower")
    p = lax.axis_index("peer")
    x, c = t // NC, t % NC
    y, z = p % NY, p // NY
    px = x % 2
    c64 = c * 64

    def peer_at(dz, dy):
        return (t, wrap(z + dz, NZ) * NY + wrap(y + dy, NY))

    def far_first(i):
        a, b = i // NY, i % NY
        ka, kb = (a + 1) // 2, (b + 1) // 2
        dz = NZ // 2 + ka * (1 - 2 * (a % 2))
        dy = NY // 2 + kb * (1 - 2 * (b % 2))
        return dz, dy

    loads = [
        (emb, embv), (lists, listv), (w2, W2.at[0, y]), (owners, ownv), (counts, cntv), (item, itemv),
    ]
    for s in range(NZ):
        zz = wrap(z + ZREL[s], NZ)
        loads.append((of.at[:, pl.ds(pl.multiple_of(zz * HZ, HZ), HZ)], ofv.at[s]))
    loads += [(cot, cotv), (ot, otv), (cd, cdv), (cu, cuv), (comp, compv)]
    copies = [pltpu.make_async_copy(a, b, lsem.at[i]) for i, (a, b) in enumerate(loads)]
    for cp in copies:
        cp.start()
    L_EMB, L_LIST, L_W2, L_OWN, L_CNT, L_ITEM, L_OF = 0, 1, 2, 3, 4, 5, 6
    L_COT, L_OT, L_CD, L_CU, L_COMP = 14, 15, 16, 17, 18

    barrier = pltpu.get_barrier_semaphore()

    def greet_peer(i, carry):
        dz, dy = far_first(i)
        pl.semaphore_signal(barrier, inc=1, device_id=peer_at(dz, dy), device_id_type=MESH)
        return carry

    lax.fori_loop(0, NP - 1, greet_peer, 0)

    def greet_tower(i, carry):
        pl.semaphore_signal(barrier, inc=1, device_id=(wrap(t + i, NT), p), device_id_type=MESH)
        return carry

    lax.fori_loop(1, NT, greet_tower, 0)

    copies[L_EMB].wait()
    copies[L_LIST].wait()
    order = listv[...]
    inner = order & (RBLK - 1)
    quarter = order >> 9
    lane = iota((32, 128), 1)

    def build_hot(k, carry):
        r0 = pl.multiple_of(k * 64, 64)
        rows = iota((64, LISTED), 0) + r0
        hot[pl.ds(r0, 64), :] = jnp.where(rows == inner, 1.0, 0.0).astype(BF16)
        return carry

    lax.fori_loop(0, RBLK // 64, build_hot, 0)
    stacked = jnp.concatenate([embv[:, k * RBLK:(k + 1) * RBLK] for k in range(FOLD)], axis=0)
    for n in range(4):
        cols = slice(n * 512, (n + 1) * 512)
        got = dot(stacked, hot[:, cols])
        q = quarter[:, cols]
        srt = jnp.where(q == 0, got[0:64], 0.0)
        for k in range(1, FOLD):
            srt = srt + jnp.where(q == k, got[k * 64:(k + 1) * 64], 0.0)
        for b in range(4):
            blk = srt[:, b * 128:(b + 1) * 128]
            both = jnp.concatenate([blk, pltpu.roll(blk, 96, 1)], axis=0)
            turned = both.T.astype(BF16)
            pay[n * 8 + b * 2] = turned[0:32]
            pay[n * 8 + b * 2 + 1] = turned[64:96]

    pl.semaphore_wait(barrier, NP - 1 + NT - 1)

    def exchange(src, dst, ssem, rsem):
        def one(i, carry):
            dz, dy = far_first(i)
            to = peer_at(dz, dy)
            pltpu.make_async_remote_copy(
                src_ref=src.at[to[1]], dst_ref=dst.at[p], send_sem=ssem, recv_sem=rsem,
                device_id=to, device_id_type=MESH,
            ).start()
            return carry

        lax.fori_loop(0, NP - 1, one, 0)
        dst[p] = src[p]

    def exchange_wait(dst, sem):
        part = dst.at[pl.ds(0, NP - 1)]
        pltpu.make_async_copy(part, part, sem).wait()

    def towers(src, dst, ssem, rsem):
        for i in range(1, NT):
            to = wrap(t + i, NT)
            pltpu.make_async_remote_copy(
                src_ref=src.at[pl.ds(pl.multiple_of(to * CAP, CAP), CAP)],
                dst_ref=dst.at[pl.ds(pl.multiple_of(t * CAP, CAP), CAP)],
                send_sem=ssem, recv_sem=rsem, device_id=(to, p), device_id_type=MESH,
            ).start()
        mine = pl.ds(pl.multiple_of(t * CAP, CAP), CAP)
        dst[mine] = src[mine]

    def towers_wait(dst, sem):
        part = dst.at[pl.ds(0, SLOTS - CAP)]
        pltpu.make_async_copy(part, part, sem).wait()

    ym, yp, yq = wrap(y - 1, NY), wrap(y + 1, NY), wrap(y + 2, NY)
    SETS = (ym, yp, yq)
    mine32 = c64 + px * 32
    sent = []

    def rcopy(src, dst, ssem, rsem, to):
        return pltpu.make_async_remote_copy(
            src_ref=src, dst_ref=dst, send_sem=ssem, recv_sem=rsem, device_id=to, device_id_type=MESH
        )

    def rows(slot, yy, r0, n):
        return W2.at[slot, yy, pl.ds(pl.multiple_of(r0, 16), n)]

    def rows_b(b, yy, r0, n):
        s0, k = BATCH[b]
        return W2.at[pl.ds(s0, k), yy, pl.ds(pl.multiple_of(r0, 16), n)]

    def z_copies():
        out = []
        for i, (a, b, r0, n, d) in enumerate((
            (0, 1, 0, 64, 1), (0, 2, 0, 64, -1), (0, 3, 0, 64, 2), (0, 4, 0, 64, -2),
            (3, 5, 0, 64, 1), (4, 6, 0, 64, -1), (3, 7, 0, 32, 2), (4, 7, 32, 32, -2),
        )):
            out.append(rcopy(rows(a, y, c64 + r0, n), rows(b, y, c64 + r0, n), zs.at[i], zr.at[i], peer_at(d, 0)))
        return out

    zc = z_copies()

    def start(cp):
        cp.start()
        sent.append(cp)

    def y1(b):
        part = rows_b(b, y, mine32, 32)
        return [rcopy(part, part, ys.at[b * 4 + i], yr.at[b * 4 + i], peer_at(0, d)) for i, d in enumerate((1, -1))]

    def y2(b):
        lo = rows_b(b, ym, mine32, 16)
        hi = rows_b(b, yp, mine32 + 16, 16)
        return [
            rcopy(lo, lo, ys.at[b * 4 + 2], yr.at[b * 4 + 2], peer_at(0, 1)),
            rcopy(hi, hi, ys.at[b * 4 + 3], yr.at[b * 4 + 3], peer_at(0, -1)),
        ]

    def xc(b, k):
        out = []
        for i, d in enumerate((1, -1)):
            part = rows_b(b, SETS[k], mine32 + 16 * i, 16)
            e = b * 6 + k * 2 + i
            out.append(rcopy(part, part, xs.at[e], xr.at[e], (wrap(x + d, NX) * NC + c, p)))
        return out

    def dc(b, k):
        part = rows_b(b, (SETS + (y,))[k], c64, 64)
        e = b * 4 + k
        return rcopy(part, part, ds.at[e], dr.at[e], (x * NC + 1 - c, p))

    def e1(b):
        for i in ((), (0, 1), (2, 3), (4, 5, 6, 7))[b]:
            zc[i].wait_recv()
        if b == 2:
            for i in (4, 5, 6, 7):
                start(zc[i])
        for cp in y1(b):
            start(cp)
        if b:
            start(dc(b, 3))

    def e2(b):
        for cp in y1(b):
            cp.wait_recv()
        for cp in y2(b):
            start(cp)
        for k in (0, 1):
            for cp in xc(b, k):
                start(cp)

    def e3(b):
        for cp in y2(b):
            cp.wait_recv()
        for cp in xc(b, 2):
            start(cp)

    def e4(b, ks):
        for k in ks:
            for cp in xc(b, k):
                cp.wait_recv()
            start(dc(b, k))

    def e5(b):
        for k in ((0, 1, 2) if b == 0 else (0, 1, 2, 3)):
            dc(b, k).wait_recv()

    exchange(pay, arr, asend, arecv)
    copies[L_W2].wait()
    for i in range(4):
        start(zc[i])
    e1(0)

    copies[L_ITEM].wait()
    for s in range(NZ):
        copies[L_OF + s].wait()

    def item_step(s, carry):
        prei[s] = dot(itemv[...], ofv[s, WIDE:, :])
        return carry

    lax.fori_loop(0, NZ, item_step, 0)
    e2(0)
    e1(1)
    e1(2)
    copies[L_COT].wait()
    copies[L_OT].wait()

    def cot_step(n, carry):
        r0 = pl.multiple_of(n * 256, 256)
        g3[:, pl.ds(r0, 256)] = dot_t(cotv[...], otv[pl.ds(r0, 256), :])
        return carry

    lax.fori_loop(0, H2 // 256, cot_step, 0)

    copies[L_OWN].wait()
    copies[L_CNT].wait()
    own = ownv[...]
    choose = jnp.where(iota((8, UDEV), 0) == own, 1.0, 0.0)
    before = jnp.where(iota((UDEV, UDEV), 0) < iota((UDEV, UDEV), 1), 1.0, 0.0).astype(BF16)
    earlier = dot(choose.astype(BF16), before)
    pos = jnp.sum(choose * earlier, axis=0, keepdims=True)
    target = own * CAP + pos.astype(jnp.int32)
    hit = iota((SLOTS, UDEV), 0) == target
    disp = jnp.where(hit, 1.0, 0.0).astype(BF16)
    held = dot(jnp.where(hit, cntv[...].astype(F32), 0.0).astype(BF16), jnp.ones((UDEV, 128), BF16))
    tsend[:, WIDE:] = held.astype(BF16)
    for i in (L_CD, L_CU, L_COMP):
        copies[i].wait()

    exchange_wait(arr, arecv)

    def lay(j, carry):
        a = arr[2 * j].astype(F32)
        b = arr[2 * j + 1].astype(F32)
        at = pl.ds(pl.multiple_of(j * 128, 128), 128)
        SR[0:32, at] = jnp.where(lane < 64, a, pltpu.roll(b, 64, 1)).astype(BF16)
        SR[32:64, at] = jnp.where(lane < 64, pltpu.roll(a, 64, 1), b).astype(BF16)
        return carry

    lax.fori_loop(0, NP // 2, lay, 0)
    low = dot(SR[...], cdv[...]).astype(BF16)
    lift[...] = dot(low, cuv[...])
    wide = SR[...].astype(F32)
    crossed = (wide * lift[...] + wide).astype(BF16)
    compressed = dot(crossed, compv[...]).astype(BF16)
    tsend[:, :WIDE] = dot(disp, compressed).astype(BF16)
    towers(tsend, trecv, tsem, trsem)

    e3(0)
    e2(1)
    e1(3)
    e2(2)
    e4(0, (0, 1, 2))

    towers_wait(trecv, trsem)
    qi = iota((ROWS, SLOTS), 0)
    si = iota((ROWS, SLOTS), 1) * MOSTC
    spread = jnp.where((qi >= si) & (qi < si + MOSTC), 1.0, 0.0).astype(BF16)
    grid = dot(spread, trecv[...])
    expanded = grid[:, :WIDE].astype(BF16)
    third = (qi * 21846) >> 16
    live = jnp.where((qi - third * MOSTC).astype(F32) < grid[:, WIDE:], 1.0, 0.0)[:, 0:1]

    def first_step(s, carry):
        pre = prei[s] + dot(expanded, ofv[s, :WIDE, :])
        sig = 0.5 * jnp.tanh(0.5 * pre) + 0.5
        act = pre * sig
        hid[s] = act.astype(BF16)
        slope[s] = (sig + act * (1.0 - sig)).astype(BF16)
        return carry

    lax.fori_loop(0, NZ, first_step, 0)

    def second(s, n, acc):
        at = pl.ds(pl.multiple_of(n * 256, 256), 256)
        w = W2[s, :, :, at].reshape(HZ, 256)
        v = dot(hid[s], w)
        if acc:
            pre2[:, at] += v
        else:
            pre2[:, at] = v

    def second_slot(s, acc):
        def step(n, carry):
            second(s, n, acc)
            return carry

        lax.fori_loop(0, 4, step, 0)

    e3(1)
    e3(2)
    e4(1, (0, 1, 2))
    e5(0)
    second_slot(0, False)
    e2(3)
    e4(2, (0, 1, 2))
    e5(1)
    second_slot(1, True)
    second_slot(2, True)
    e3(3)
    e5(2)
    second_slot(3, True)
    second_slot(4, True)
    e4(3, (0, 1, 2))
    e5(3)
    for s in (5, 6, 7):
        second_slot(s, True)

    def mid_step(n, carry):
        at = pl.ds(pl.multiple_of(n * 256, 256), 256)
        pre = pre2[:, at]
        sig = 0.5 * jnp.tanh(0.5 * pre) + 0.5
        act = pre * sig
        hs[:, at] = act.astype(BF16)
        gs2[:, at] = (g3[:, at] * live * (sig + act * (1.0 - sig))).astype(BF16)
        return carry

    lax.fori_loop(0, 4, mid_step, 0)
    sacc[...] = jnp.zeros_like(sacc)

    def back_step(s, carry):
        w = W2[s].reshape(HZ, H2)
        g = (dot_t(gs2[...], w) * slope[s].astype(F32)).astype(BF16)
        sacc[...] += dot_t(g, ofv[s, :WIDE, :])
        return carry

    lax.fori_loop(0, NZ, back_step, 0)
    qj = iota((SLOTS, ROWS), 1)
    sj = iota((SLOTS, ROWS), 0) * MOSTC
    gather3 = jnp.where((qj >= sj) & (qj < sj + MOSTC), 1.0, 0.0).astype(BF16)
    gsend[...] = dot(gather3, sacc[...].astype(BF16)).astype(BF16)
    towers(gsend, grecv, gsem, grsem)

    def out_step(n, carry):
        at = pl.ds(pl.multiple_of(n * 256, 256), 256)
        outv[:, at] = (dot(hs[...], otv[:, at]) * live).astype(BF16)
        return carry

    lax.fori_loop(0, 4, out_step, 0)
    out_copy = pltpu.make_async_copy(outv, out_hbm, lsem.at[19])
    out_copy.start()

    towers_wait(grecv, grsem)
    eye = jnp.where(iota((UDEV, UDEV), 0) == iota((UDEV, UDEV), 1), 1.0, 0.0).astype(BF16)
    undisp = dot_t(eye, disp).astype(BF16)
    session_grad = dot(undisp, grecv[...]).astype(BF16)
    gc = dot_t(session_grad, compv[...]).astype(BF16).astype(F32)
    gl = (gc * SR[...].astype(F32)).astype(BF16)
    glow = dot_t(gl, cuv[...]).astype(BF16)
    lift[...] = gc * (lift[...] + 1.0) + dot_t(glow, cdv[...])

    def unlay(j, carry):
        at = pl.ds(pl.multiple_of(j * 128, 128), 128)
        lo = lift[0:32, at]
        hi = lift[32:64, at]
        bpay[2 * j] = jnp.where(lane < 64, lo, pltpu.roll(hi, 64, 1)).astype(BF16)
        bpay[2 * j + 1] = jnp.where(lane < 64, pltpu.roll(lo, 64, 1), hi).astype(BF16)
        return carry

    lax.fori_loop(0, NP // 2, unlay, 0)
    exchange(bpay, barr, bsend, brecv)
    for cp in sent:
        cp.wait_send()
    exchange_wait(pay, asend)
    towers_wait(tsend, tsem)
    towers_wait(gsend, gsem)
    exchange_wait(barr, brecv)

    total = jnp.zeros((FOLD * 64, RBLK), F32)
    zero = jnp.zeros((32, 128), F32)
    lane64 = iota((64, 128), 1) & 63
    for n in range(4):
        parts = []
        for b in range(4):
            p0 = n * 8 + b * 2
            tall = jnp.concatenate([barr[p0].astype(F32), zero, barr[p0 + 1].astype(F32), zero], axis=0)
            turned = tall.T
            parts.append(jnp.where(lane64 < 32, turned[0:64], pltpu.roll(turned[64:128], 32, 1)))
        grads = jnp.concatenate(parts, axis=1)
        q = quarter[:, n * 512:(n + 1) * 512]
        laid = jnp.concatenate([jnp.where(q == k, grads, 0.0).astype(BF16) for k in range(FOLD)], axis=0)
        total = total + dot_t(laid, hot[:, n * 512:(n + 1) * 512])
    for k in range(FOLD):
        egv[:, k * RBLK:(k + 1) * RBLK] = total[k * 64:(k + 1) * 64].astype(BF16)
    eg_copy = pltpu.make_async_copy(egv, eg_hbm, lsem.at[20])
    eg_copy.start()
    exchange_wait(bpay, bsend)
    out_copy.wait()
    eg_copy.wait()


def body(
    embeddings, session_lists, owners, counts, item_feats, cotangent,
    cross_down, cross_up, compress, over_first, over_second, over_third,
):
    dma = pltpu.SemaphoreType.DMA
    vm = pltpu.VMEM
    scratch = [
        vm((64, LISTED), BF16), vm((1, LISTED), jnp.int32), vm((1, UDEV), jnp.int32), vm((1, UDEV), jnp.int32),
        vm((ROWS, WIDE), BF16), vm((ROWS, H2), BF16), vm((FEAT, WIDE), BF16), vm((WIDE, FEAT), BF16),
        vm((FEAT, WIDE), BF16), vm((NZ, 2 * WIDE, HZ), BF16), vm((NZ, NY, HS, H2), BF16), vm((H2, H2), BF16),
        vm((RBLK, LISTED), BF16), vm((NP, 32, 128), BF16), vm((NP, 32, 128), BF16), vm((UDEV, FEAT), BF16),
        vm((UDEV, FEAT), F32), vm((SLOTS, WIDE + 128), BF16), vm((SLOTS, WIDE + 128), BF16),
        vm((SLOTS, WIDE), BF16), vm((SLOTS, WIDE), BF16), vm((NP, 32, 128), BF16), vm((NP, 32, 128), BF16),
        vm((64, LISTED), BF16),
        vm((NZ, ROWS, HZ), F32), vm((NZ, ROWS, HZ), BF16), vm((NZ, ROWS, HZ), BF16), vm((ROWS, H2), F32),
        vm((ROWS, H2), F32), vm((ROWS, H2), BF16), vm((ROWS, H2), BF16), vm((ROWS, H2), BF16), vm((ROWS, WIDE), F32),
        dma((21,)), dma, dma, dma, dma, dma, dma, dma, dma,
        dma((8,)), dma((8,)), dma((16,)), dma((16,)), dma((24,)), dma((24,)), dma((16,)), dma((16,)),
    ]
    anywhere = pl.BlockSpec(memory_space=pl.ANY)
    over_out, emb_grad_t = pl.pallas_call(
        kernel,
        out_shape=(
            jax.ShapeDtypeStruct((ROWS, H2), BF16),
            jax.ShapeDtypeStruct((64, LISTED), BF16),
        ),
        in_specs=[anywhere] * 12,
        out_specs=(anywhere, anywhere),
        scratch_shapes=scratch,
        compiler_params=pltpu.CompilerParams(
            collective_id=0, has_side_effects=True, vmem_limit_bytes=60 * 2**20
        ),
    )(
        embeddings.T, session_lists, owners.reshape(1, UDEV), counts.reshape(1, UDEV), item_feats, cotangent,
        cross_down, cross_up, compress, over_first, over_second, over_third,
    )
    return over_out, emb_grad_t.T


def solution(mesh):
    return jax.shard_map(
        body,
        mesh=mesh,
        in_specs=(
            P("tower", "peer"),
            P("tower", None),
            P(("tower", "peer"), None),
            P(("tower", "peer")),
            P(("tower", "peer"), None),
            P(("tower", "peer"), None),
            P(),
            P(),
            P(),
            P(),
            P("peer", None),
            P(),
        ),
        out_specs=(P(("tower", "peer"), None), P("tower", "peer")),
        check_vma=False,
    )
```

time: 188 us -> 88.9 us (0.47)
  Pallas kernels: 0 us -> 84.4 us
  waiting for transfers between devices: 63.1 us -> 0 us
  matrix products: 40.1 us -> 0 us
  starting transfers between devices: 28.4 us -> 0 us
  local copies, waits for them, and re-layouts: 23.3 us -> 3.73 us
  between operations: 14.2 us -> 0.64 us
  blocking collectives: 11 us -> 0 us
  other arithmetic: 6.42 us -> 0 us
    pallas_call x0 -> x1, Pallas kernels: none -> 84.4 us  [body(): pl.pallas_call(kernel, out_shape=(jax.ShapeDtypeStruct((ROWS, H2), BF16),...]
    dot_general x9 -> x0, matrix products: 40.1 us -> none  [the longest x4 18 us: times_t(): lax.dot_general(left, right, (((1,), (1,)), ((), ())), preferred_element_...]
    all_gather x1 -> x0, waiting for transfers between devices: 36.3 us -> none  [body(): lax.all_gather(over_second, 'peer', axis=0, tiled=True)]
    all_to_all x4 -> x0, starting transfers between devices: 28.4 us -> none  [the longest x1 10.6 us: body(): lax.all_to_all(picked, 'peer', split_axis=0, concat_axis=1, tiled=True)]
    all_to_all x4 -> x0, waiting for transfers between devices: 26.2 us -> none  [the longest x1 13.4 us: body(): lax.all_to_all(picked, 'peer', split_axis=0, concat_axis=1, tiled=True)]
    all_to_all x1 -> x0, blocking collectives: 11 us -> none  [body(): lax.all_to_all(sample_grad.reshape(towers, slots * MOSTC, comp_width), 't...]
    gather x1 -> x0, local copies, waits for them, and re-layouts: 6.18 us -> none  [body(): picked = jnp.take(embeddings, order, axis=0)]
    scatter x1 -> x0, local copies, waits for them, and re-layouts: 5.87 us -> none  [body(): emb_grad = jnp.zeros_like(embeddings).at[order].set(columns_back)]
  transfers between devices with their start and end apart: 5 -> 0, of which waited for: 4 -> 0; matrix products, arithmetic and copies ran while one was open for 17% -> 0% of each run, Pallas kernels for 0% -> 0%
where the time goes in v1:
time: 88.9 us; the launch traced here: 88.7 us
  Pallas kernels  84.4 us (95%)
  local copies, waits for them, and re-layouts  3.73 us (4%)
    pallas_call x1, Pallas kernels, body(): pl.pallas_call(kernel, out_shape=(jax.ShapeDtypeStruct((ROWS, H2), BF16),...  84.4 us
    unnamed x2, local copies, waits for them, and re-layouts  3.73 us

profile of v1, /device:TPU:1, one launch (start us, length us, event | category | flops | bytes accessed | tf_op | source)
XLA Modules:
  0.0 88.7 jit_solution(6788761255626556130)
XLA Ops:
  0.6 84.4 %shard_map.131 = (bf16[384,1024]{1,0:T(8,128)(2,1)}, bf16[64,2048]{1,0:T(8,128)(2,1)}) custom-call(bf16[64,2048]{1,0:T(8,128)(2,1)} %bitcast.4, s32[1,2048]{1,0:T(1,128)} %lists.1, s32[1,64]{1,0:T(1,128)} %bitcast.6, s32[1,64]{1,0:T(1,128)} %bitcast.7, bf16[384,256]{1,0:T(8,128)(2,1)} %item.1, bf16[384,1024]{1,0:T(8,128)(2,1)} %cot.1, bf16[2048,256]{1,0:T(8,128)(2,1)} %cd.1, ...), custom_call_target="tpu_custom_call" | custom-call | tf_op jit(solution)/shard_map/pallas_call | solution.py:477
  85.0 2.1 %copy.16 = bf16[384,1024]{1,0:T(8,128)(2,1)} copy(bf16[384,1024]{1,0:T(8,128)(2,1)} %get-tuple-element.8) | data formatting | bytes 1572864
  87.1 1.7 %copy.17 = bf16[2048,64]{0,1:T(8,128)(2,1)} copy(bf16[2048,64]{0,1:T(8,128)(2,1)} %bitcast.5) | data formatting | bytes 524288

commit v2 on v1

--- a/solution.py
+++ b/solution.py
@@ -19,8 +19,10 @@
 LISTED = UDEV * NP
 FOLD = 4
 RBLK = LISTED // FOLD
-ZREL = (0, 7, 1, 6, 2, 5, 3, 4)
-BATCH = ((0, 1), (1, 2), (3, 2), (5, 3))
+ZREL = (0, 4, 7, 1, 6, 2, 5, 3)
+BATCH = ((0, 1), (2, 2), (4, 2), (6, 2), (1, 1))
+PAIRS = NZ // 2
+HP = 2 * HZ
 
 
 def dot(a, b):
@@ -70,7 +72,8 @@
     ]
     for s in range(NZ):
         zz = wrap(z + ZREL[s], NZ)
-        loads.append((of.at[:, pl.ds(pl.multiple_of(zz * HZ, HZ), HZ)], ofv.at[s]))
+        part = ofv.at[s // 2, :, pl.ds((s % 2) * HZ, HZ)]
+        loads.append((of.at[:, pl.ds(pl.multiple_of(zz * HZ, HZ), HZ)], part))
     loads += [(cot, cotv), (ot, otv), (cd, cdv), (cu, cuv), (comp, compv)]
     copies = [pltpu.make_async_copy(a, b, lsem.at[i]) for i, (a, b) in enumerate(loads)]
     for cp in copies:
@@ -157,125 +160,130 @@
         pltpu.make_async_copy(part, part, sem).wait()
 
     ym, yp, yq = wrap(y - 1, NY), wrap(y + 1, NY), wrap(y + 2, NY)
-    SETS = (ym, yp, yq)
-    mine32 = c64 + px * 32
+    SETS = (ym, yp, yq, y)
+    near = c64 + px * 32
+    other = c64 + (1 - px) * 32
     sent = []
+
+    def start(cp):
+        cp.start()
+        sent.append(cp)
 
     def rcopy(src, dst, ssem, rsem, to):
         return pltpu.make_async_remote_copy(
             src_ref=src, dst_ref=dst, send_sem=ssem, recv_sem=rsem, device_id=to, device_id_type=MESH
         )
 
-    def rows(slot, yy, r0, n):
-        return W2.at[slot, yy, pl.ds(pl.multiple_of(r0, 16), n)]
-
-    def rows_b(b, yy, r0, n):
-        s0, k = BATCH[b]
-        return W2.at[pl.ds(s0, k), yy, pl.ds(pl.multiple_of(r0, 16), n)]
-
-    def z_copies():
-        out = []
-        for i, (a, b, r0, n, d) in enumerate((
-            (0, 1, 0, 64, 1), (0, 2, 0, 64, -1), (0, 3, 0, 64, 2), (0, 4, 0, 64, -2),
-            (3, 5, 0, 64, 1), (4, 6, 0, 64, -1), (3, 7, 0, 32, 2), (4, 7, 32, 32, -2),
-        )):
-            out.append(rcopy(rows(a, y, c64 + r0, n), rows(b, y, c64 + r0, n), zs.at[i], zr.at[i], peer_at(d, 0)))
-        return out
-
-    zc = z_copies()
-
-    def start(cp):
-        cp.start()
-        sent.append(cp)
+    def rows(slot, r0, n):
+        return W2.at[slot, y, pl.ds(pl.multiple_of(near + r0, 16), n)]
+
+    def rows_b(b, k, r0, n):
+        s0, m = BATCH[b]
+        return W2.at[pl.ds(s0, m), SETS[k], pl.ds(pl.multiple_of(r0, 16), n)]
+
+    def zc(i):
+        a, b, r0, n, d = (
+            (0, 2, 0, 32, 1), (0, 3, 0, 32, -1), (0, 4, 0, 32, 2), (0, 5, 0, 32, -2),
+            (4, 6, 0, 32, 1), (5, 7, 0, 32, -1), (4, 1, 0, 16, 2), (5, 1, 16, 16, -2),
+        )[i]
+        return rcopy(rows(a, r0, n), rows(b, r0, n), zs.at[i], zr.at[i], peer_at(d, 0))
+
+    def same(part, ssem, rsem, e, to):
+        return rcopy(part, part, ssem.at[e], rsem.at[e], to)
 
     def y1(b):
-        part = rows_b(b, y, mine32, 32)
-        return [rcopy(part, part, ys.at[b * 4 + i], yr.at[b * 4 + i], peer_at(0, d)) for i, d in enumerate((1, -1))]
+        return [same(rows_b(b, 3, near, 32), ys, yr, b * 4 + i, peer_at(0, d)) for i, d in enumerate((1, -1))]
 
     def y2(b):
-        lo = rows_b(b, ym, mine32, 16)
-        hi = rows_b(b, yp, mine32 + 16, 16)
+        return [same(rows_b(b, i, near + 16 * i, 16), ys, yr, b * 4 + 2 + i, peer_at(0, d)) for i, d in enumerate((1, -1))]
+
+    def xc(b, k):
         return [
-            rcopy(lo, lo, ys.at[b * 4 + 2], yr.at[b * 4 + 2], peer_at(0, 1)),
-            rcopy(hi, hi, ys.at[b * 4 + 3], yr.at[b * 4 + 3], peer_at(0, -1)),
+            same(rows_b(b, k, near + 16 * i, 16), xs, xr, b * 8 + k * 2 + i, (wrap(x + d, NX) * NC + c, p))
+            for i, d in enumerate((1, -1))
         ]
 
-    def xc(b, k):
-        out = []
-        for i, d in enumerate((1, -1)):
-            part = rows_b(b, SETS[k], mine32 + 16 * i, 16)
-            e = b * 6 + k * 2 + i
-            out.append(rcopy(part, part, xs.at[e], xr.at[e], (wrap(x + d, NX) * NC + c, p)))
-        return out
-
-    def dc(b, k):
-        part = rows_b(b, (SETS + (y,))[k], c64, 64)
-        e = b * 4 + k
-        return rcopy(part, part, ds.at[e], dr.at[e], (x * NC + 1 - c, p))
-
-    def e1(b):
-        for i in ((), (0, 1), (2, 3), (4, 5, 6, 7))[b]:
-            zc[i].wait_recv()
+    def dc(b, k, o):
+        return same(rows_b(b, k, other if o else near, 32), ds, dr, b * 8 + k * 2 + o, (x * NC + 1 - c, p))
+
+    def own(b):
+        for cp in y1(b) + xc(b, 3):
+            start(cp)
+        start(dc(b, 3, 0))
+
+    def ez(b):
+        for i in ((), (0, 1), (2, 3), (4, 5), (6, 7))[b]:
+            zc(i).wait_recv()
         if b == 2:
             for i in (4, 5, 6, 7):
-                start(zc[i])
-        for cp in y1(b):
-            start(cp)
-        if b:
-            start(dc(b, 3))
-
-    def e2(b):
+                start(zc(i))
+        own(b)
+
+    def ey(b):
         for cp in y1(b):
             cp.wait_recv()
-        for cp in y2(b):
+        for cp in y2(b) + xc(b, 0) + xc(b, 1):
             start(cp)
         for k in (0, 1):
-            for cp in xc(b, k):
-                start(cp)
-
-    def e3(b):
+            start(dc(b, k, 0))
+
+    def ey2(b):
         for cp in y2(b):
             cp.wait_recv()
         for cp in xc(b, 2):
             start(cp)
-
-    def e4(b, ks):
+        start(dc(b, 2, 0))
+
+    def ex(b, *ks):
         for k in ks:
             for cp in xc(b, k):
                 cp.wait_recv()
-            start(dc(b, k))
-
-    def e5(b):
-        for k in ((0, 1, 2) if b == 0 else (0, 1, 2, 3)):
-            dc(b, k).wait_recv()
-
+            start(dc(b, k, 1))
+
+    def ed(b):
+        for k in range(4 if b else 3):
+            for o in (0, 1):
+                dc(b, k, o).wait_recv()
+
+    copies[L_W2].wait()
+    for i in (0, 1):
+        start(zc(i))
+    for cp in y1(0):
+        start(cp)
+    for i in (2, 3):
+        start(zc(i))
     exchange(pay, arr, asend, arecv)
-    copies[L_W2].wait()
-    for i in range(4):
-        start(zc[i])
-    e1(0)
 
     copies[L_ITEM].wait()
     for s in range(NZ):
         copies[L_OF + s].wait()
 
-    def item_step(s, carry):
-        prei[s] = dot(itemv[...], ofv[s, WIDE:, :])
-        return carry
-
-    lax.fori_loop(0, NZ, item_step, 0)
-    e2(0)
-    e1(1)
-    e1(2)
+    def item_step(q, carry):
+        for h in (slice(0, HZ), slice(HZ, HP)):
+            prei[q, :, h] = dot(itemv[...], ofv[q, WIDE:, h])
+        return carry
+
+    lax.fori_loop(0, PAIRS // 2, item_step, 0)
+    ez(1)
+    ey(0)
+    lax.fori_loop(PAIRS // 2, PAIRS, item_step, 0)
+    ez(2)
+    ey2(0)
+    ey(1)
     copies[L_COT].wait()
     copies[L_OT].wait()
 
     def cot_step(n, carry):
-        r0 = pl.multiple_of(n * 256, 256)
-        g3[:, pl.ds(r0, 256)] = dot_t(cotv[...], otv[pl.ds(r0, 256), :])
-        return carry
-
-    lax.fori_loop(0, H2 // 256, cot_step, 0)
+        r0 = pl.multiple_of(n * 512, 512)
+        g3[:, pl.ds(r0, 512)] = dot_t(cotv[...], otv[pl.ds(r0, 512), :])
+        return carry
+
+    lax.fori_loop(0, 2, cot_step, 0)
+    ez(3)
+    ez(4)
+    ey(2)
+    ex(1, 3)
+    ex(0, 0, 1)
 
     copies[L_OWN].wait()
     copies[L_CNT].wait()
@@ -311,11 +319,17 @@
     tsend[:, :WIDE] = dot(disp, compressed).astype(BF16)
     towers(tsend, trecv, tsem, trsem)
 
-    e3(0)
-    e2(1)
-    e1(3)
-    e2(2)
-    e4(0, (0, 1, 2))
+    ey2(1)
+    ex(2, 3)
+    ex(0, 2)
+    ey(3)
+    ey(4)
+    ey2(2)
+    ex(1, 0, 1)
+    ey2(3)
+    ey2(4)
+    ex(3, 3)
+    ex(4, 3)
 
     towers_wait(trecv, trsem)
     qi = iota((ROWS, SLOTS), 0)
@@ -326,50 +340,36 @@
     third = (qi * 21846) >> 16
     live = jnp.where((qi - third * MOSTC).astype(F32) < grid[:, WIDE:], 1.0, 0.0)[:, 0:1]
 
-    def first_step(s, carry):
-        pre = prei[s] + dot(expanded, ofv[s, :WIDE, :])
-        sig = 0.5 * jnp.tanh(0.5 * pre) + 0.5
-        act = pre * sig
-        hid[s] = act.astype(BF16)
-        slope[s] = (sig + act * (1.0 - sig)).astype(BF16)
-        return carry
-
-    lax.fori_loop(0, NZ, first_step, 0)
-
-    def second(s, n, acc):
-        at = pl.ds(pl.multiple_of(n * 256, 256), 256)
-        w = W2[s, :, :, at].reshape(HZ, 256)
-        v = dot(hid[s], w)
-        if acc:
-            pre2[:, at] += v
-        else:
-            pre2[:, at] = v
-
-    def second_slot(s, acc):
-        def step(n, carry):
-            second(s, n, acc)
-            return carry
-
-        lax.fori_loop(0, 4, step, 0)
-
-    e3(1)
-    e3(2)
-    e4(1, (0, 1, 2))
-    e5(0)
-    second_slot(0, False)
-    e2(3)
-    e4(2, (0, 1, 2))
-    e5(1)
-    second_slot(1, True)
-    second_slot(2, True)
-    e3(3)
-    e5(2)
-    second_slot(3, True)
-    second_slot(4, True)
-    e4(3, (0, 1, 2))
-    e5(3)
-    for s in (5, 6, 7):
-        second_slot(s, True)
+    def first_step(q, carry):
+        for h in (slice(0, HZ), slice(HZ, HP)):
+            pre = prei[q, :, h] + dot(expanded, ofv[q, :WIDE, h])
+            sig = 0.5 * jnp.tanh(0.5 * pre) + 0.5
+            act = pre * sig
+            hid[q, :, h] = act.astype(BF16)
+            slope[q, :, h] = (sig + act * (1.0 - sig)).astype(BF16)
+        return carry
+
+    def pair(q):
+        return W2[pl.ds(2 * q, 2)].reshape(HP, H2)
+
+    lax.fori_loop(0, PAIRS // 2, first_step, 0)
+    ex(1, 2)
+    ex(2, 0, 1)
+    ex(2, 2)
+    lax.fori_loop(PAIRS // 2, PAIRS, first_step, 0)
+    ex(3, 0, 1)
+    ex(4, 0, 1)
+    ed(1)
+    pre2[...] = dot(hid[1], pair(1))
+    ex(3, 2)
+    ex(4, 2)
+    ed(2)
+    pre2[...] += dot(hid[2], pair(2))
+    ed(3)
+    pre2[...] += dot(hid[3], pair(3))
+    ed(0)
+    ed(4)
+    pre2[...] += dot(hid[0], pair(0))
 
     def mid_step(n, carry):
         at = pl.ds(pl.multiple_of(n * 256, 256), 256)
@@ -383,13 +383,12 @@
     lax.fori_loop(0, 4, mid_step, 0)
     sacc[...] = jnp.zeros_like(sacc)
 
-    def back_step(s, carry):
-        w = W2[s].reshape(HZ, H2)
-        g = (dot_t(gs2[...], w) * slope[s].astype(F32)).astype(BF16)
-        sacc[...] += dot_t(g, ofv[s, :WIDE, :])
-        return carry
-
-    lax.fori_loop(0, NZ, back_step, 0)
+    def back_step(q, carry):
+        g = (dot_t(gs2[...], pair(q)) * slope[q].astype(F32)).astype(BF16)
+        sacc[...] += dot_t(g, ofv[q, :WIDE, :])
+        return carry
+
+    lax.fori_loop(0, PAIRS, back_step, 0)
     qj = iota((SLOTS, ROWS), 1)
     sj = iota((SLOTS, ROWS), 0) * MOSTC
     gather3 = jnp.where((qj >= sj) & (qj < sj + MOSTC), 1.0, 0.0).astype(BF16)
@@ -463,15 +462,15 @@
     scratch = [
         vm((64, LISTED), BF16), vm((1, LISTED), jnp.int32), vm((1, UDEV), jnp.int32), vm((1, UDEV), jnp.int32),
         vm((ROWS, WIDE), BF16), vm((ROWS, H2), BF16), vm((FEAT, WIDE), BF16), vm((WIDE, FEAT), BF16),
-        vm((FEAT, WIDE), BF16), vm((NZ, 2 * WIDE, HZ), BF16), vm((NZ, NY, HS, H2), BF16), vm((H2, H2), BF16),
+        vm((FEAT, WIDE), BF16), vm((PAIRS, 2 * WIDE, HP), BF16), vm((NZ, NY, HS, H2), BF16), vm((H2, H2), BF16),
         vm((RBLK, LISTED), BF16), vm((NP, 32, 128), BF16), vm((NP, 32, 128), BF16), vm((UDEV, FEAT), BF16),
         vm((UDEV, FEAT), F32), vm((SLOTS, WIDE + 128), BF16), vm((SLOTS, WIDE + 128), BF16),
         vm((SLOTS, WIDE), BF16), vm((SLOTS, WIDE), BF16), vm((NP, 32, 128), BF16), vm((NP, 32, 128), BF16),
         vm((64, LISTED), BF16),
-        vm((NZ, ROWS, HZ), F32), vm((NZ, ROWS, HZ), BF16), vm((NZ, ROWS, HZ), BF16), vm((ROWS, H2), F32),
+        vm((PAIRS, ROWS, HP), F32), vm((PAIRS, ROWS, HP), BF16), vm((PAIRS, ROWS, HP), BF16), vm((ROWS, H2), F32),
         vm((ROWS, H2), F32), vm((ROWS, H2), BF16), vm((ROWS, H2), BF16), vm((ROWS, H2), BF16), vm((ROWS, WIDE), F32),
         dma((21,)), dma, dma, dma, dma, dma, dma, dma, dma,
-        dma((8,)), dma((8,)), dma((16,)), dma((16,)), dma((24,)), dma((24,)), dma((16,)), dma((16,)),
+        dma((8,)), dma((8,)), dma((20,)), dma((20,)), dma((40,)), dma((40,)), dma((40,)), dma((40,)),
     ]
     anywhere = pl.BlockSpec(memory_space=pl.ANY)
     over_out, emb_grad_t = pl.pallas_call(

time: 88.9 us -> 78.1 us (0.88)
  Pallas kernels: 84.4 us -> 73.6 us
    pallas_call x1, Pallas kernels: 84.4 us -> 73.6 us  [body(): pl.pallas_call(kernel, out_shape=(jax.ShapeDtypeStruct((ROWS, H2), BF16),...]
where the time goes in v2:
time: 78.1 us; the launch traced here: 77.9 us
  Pallas kernels  73.6 us (94%)
  local copies, waits for them, and re-layouts  3.73 us (5%)
    pallas_call x1, Pallas kernels, body(): pl.pallas_call(kernel, out_shape=(jax.ShapeDtypeStruct((ROWS, H2), BF16),...  73.6 us
    unnamed x2, local copies, waits for them, and re-layouts  3.73 us

profile of v2, /device:TPU:1, one launch (start us, length us, event | category | flops | bytes accessed | tf_op | source)
XLA Modules:
  0.0 77.9 jit_solution(8131003757626527035)
XLA Ops:
  0.6 73.6 %shard_map.131 = (bf16[384,1024]{1,0:T(8,128)(2,1)}, bf16[64,2048]{1,0:T(8,128)(2,1)}) custom-call(bf16[64,2048]{1,0:T(8,128)(2,1)} %bitcast.4, s32[1,2048]{1,0:T(1,128)} %lists.1, s32[1,64]{1,0:T(1,128)} %bitcast.6, s32[1,64]{1,0:T(1,128)} %bitcast.7, bf16[384,256]{1,0:T(8,128)(2,1)} %item.1, bf16[384,1024]{1,0:T(8,128)(2,1)} %cot.1, bf16[2048,256]{1,0:T(8,128)(2,1)} %cd.1, ...), custom_call_target="tpu_custom_call" | custom-call | tf_op jit(solution)/shard_map/pallas_call | solution.py:476
  74.2 2.1 %copy.16 = bf16[384,1024]{1,0:T(8,128)(2,1)} copy(bf16[384,1024]{1,0:T(8,128)(2,1)} %get-tuple-element.8) | data formatting | bytes 1572864
  76.3 1.7 %copy.17 = bf16[2048,64]{0,1:T(8,128)(2,1)} copy(bf16[2048,64]{0,1:T(8,128)(2,1)} %bitcast.5) | data formatting | bytes 524288

commit v3 on v2

--- a/solution.py
+++ b/solution.py
@@ -48,7 +48,7 @@
     hot, pay, arr, SR, lift, tsend, trecv, gsend, grecv, bpay, barr, egv,
     prei, hid, slope, pre2, g3, hs, gs2, outv, sacc,
     lsem, asend, arecv, tsem, trsem, gsem, grsem, bsend, brecv,
-    zs, zr, ys, yr, xs, xr, ds, dr,
+    zs, zr, ys, yr, xs, xr, ds, dr, hop1, hop2,
 ):
     t = lax.axis_index("tower")
     p = lax.axis_index("peer")
@@ -67,8 +67,20 @@
         dy = NY // 2 + kb * (1 - 2 * (b % 2))
         return dz, dy
 
+    barrier = pltpu.get_barrier_semaphore()
+
+    close = tuple(peer_at(d, 0) for d in (-1, 1, -2, 2))
+    for to in close + tuple(peer_at(0, d) for d in (-1, 1, 2)):
+        pl.semaphore_signal(barrier, inc=1, device_id=to, device_id_type=MESH)
+
+    def greet_tower(i, carry):
+        pl.semaphore_signal(barrier, inc=1, device_id=(wrap(t + i, NT), p), device_id_type=MESH)
+        return carry
+
+    lax.fori_loop(1, NT, greet_tower, 0)
+
     loads = [
-        (emb, embv), (lists, listv), (w2, W2.at[0, y]), (owners, ownv), (counts, cntv), (item, itemv),
+        (w2, W2.at[0, y]), (emb, embv), (lists, listv), (owners, ownv), (counts, cntv), (item, itemv),
     ]
     for s in range(NZ):
         zz = wrap(z + ZREL[s], NZ)
@@ -78,23 +90,137 @@
     copies = [pltpu.make_async_copy(a, b, lsem.at[i]) for i, (a, b) in enumerate(loads)]
     for cp in copies:
         cp.start()
-    L_EMB, L_LIST, L_W2, L_OWN, L_CNT, L_ITEM, L_OF = 0, 1, 2, 3, 4, 5, 6
+    L_W2, L_EMB, L_LIST, L_OWN, L_CNT, L_ITEM, L_OF = 0, 1, 2, 3, 4, 5, 6
     L_COT, L_OT, L_CD, L_CU, L_COMP = 14, 15, 16, 17, 18
 
-    barrier = pltpu.get_barrier_semaphore()
-
-    def greet_peer(i, carry):
-        dz, dy = far_first(i)
-        pl.semaphore_signal(barrier, inc=1, device_id=peer_at(dz, dy), device_id_type=MESH)
-        return carry
-
-    lax.fori_loop(0, NP - 1, greet_peer, 0)
-
-    def greet_tower(i, carry):
-        pl.semaphore_signal(barrier, inc=1, device_id=(wrap(t + i, NT), p), device_id_type=MESH)
-        return carry
-
-    lax.fori_loop(1, NT, greet_tower, 0)
+    def exchange(src, dst, ssem, rsem):
+        def one(i, carry):
+            dz, dy = far_first(i)
+            to = peer_at(dz, dy)
+            pltpu.make_async_remote_copy(
+                src_ref=src.at[to[1]], dst_ref=dst.at[p], send_sem=ssem, recv_sem=rsem,
+                device_id=to, device_id_type=MESH,
+            ).start()
+            return carry
+
+        lax.fori_loop(0, NP - 1, one, 0)
+        dst[p] = src[p]
+
+    def exchange_wait(dst, sem):
+        part = dst.at[pl.ds(0, NP - 1)]
+        pltpu.make_async_copy(part, part, sem).wait()
+
+    def towers(src, dst, ssem, rsem):
+        for i in range(1, NT):
+            to = wrap(t + i, NT)
+            pltpu.make_async_remote_copy(
+                src_ref=src.at[pl.ds(pl.multiple_of(to * CAP, CAP), CAP)],
+                dst_ref=dst.at[pl.ds(pl.multiple_of(t * CAP, CAP), CAP)],
+                send_sem=ssem, recv_sem=rsem, device_id=(to, p), device_id_type=MESH,
+            ).start()
+        mine = pl.ds(pl.multiple_of(t * CAP, CAP), CAP)
+        dst[mine] = src[mine]
+
+    def towers_wait(dst, sem):
+        part = dst.at[pl.ds(0, SLOTS - CAP)]
+        pltpu.make_async_copy(part, part, sem).wait()
+
+    ym, yp, yq = wrap(y - 1, NY), wrap(y + 1, NY), wrap(y + 2, NY)
+    SETS = (ym, yp, yq, y)
+    near = c64 + px * 32
+    other = c64 + (1 - px) * 32
+    sent = []
+
+    def start(cp):
+        cp.start()
+        sent.append(cp)
+
+    def rcopy(src, dst, ssem, rsem, to):
+        return pltpu.make_async_remote_copy(
+            src_ref=src, dst_ref=dst, send_sem=ssem, recv_sem=rsem, device_id=to, device_id_type=MESH
+        )
+
+    def rows(slot, r0, n):
+        return W2.at[slot, y, pl.ds(pl.multiple_of(near + r0, 16), n)]
+
+    def rows_b(b, k, r0, n):
+        s0, m = BATCH[b]
+        return W2.at[pl.ds(s0, m), SETS[k], pl.ds(pl.multiple_of(r0, 16), n)]
+
+    def zc(i):
+        a, b, r0, n, d = (
+            (0, 2, 0, 32, 1), (0, 3, 0, 32, -1), (0, 4, 0, 32, 2), (0, 5, 0, 32, -2),
+            (4, 6, 0, 32, 1), (5, 7, 0, 32, -1), (4, 1, 0, 16, 2), (5, 1, 16, 16, -2),
+        )[i]
+        return rcopy(rows(a, r0, n), rows(b, r0, n), zs.at[i], zr.at[i], peer_at(d, 0))
+
+    def same(part, ssem, rsem, e, to):
+        return rcopy(part, part, ssem.at[e], rsem.at[e], to)
+
+    def y1(b):
+        return [same(rows_b(b, 3, near, 32), ys, yr, b * 4 + i, peer_at(0, d)) for i, d in enumerate((1, -1))]
+
+    def y2(b):
+        return [same(rows_b(b, i, near + 16 * i, 16), ys, yr, b * 4 + 2 + i, peer_at(0, d)) for i, d in enumerate((1, -1))]
+
+    def xc(b, k):
+        return [
+            same(rows_b(b, k, near + 16 * i, 16), xs, xr, b * 8 + k * 2 + i, (wrap(x + d, NX) * NC + c, p))
+            for i, d in enumerate((1, -1))
+        ]
+
+    def dc(b, k, o):
+        return same(rows_b(b, k, other if o else near, 32), ds, dr, b * 8 + k * 2 + o, (x * NC + 1 - c, p))
+
+    def own(b):
+        for cp in y1(b) + xc(b, 3):
+            start(cp)
+        start(dc(b, 3, 0))
+
+    def ez(b):
+        for i in ((), (0, 1), (2, 3), (4, 5), (6, 7))[b]:
+            zc(i).wait_recv()
+        if b == 2:
+            for i in (4, 5, 6, 7):
+                start(zc(i))
+        own(b)
+
+    def ey(b):
+        for cp in y1(b):
+            cp.wait_recv()
+        for cp in y2(b) + xc(b, 0) + xc(b, 1):
+            start(cp)
+        for k in (0, 1):
+            start(dc(b, k, 0))
+
+    def ey2(b):
+        for cp in y2(b):
+            cp.wait_recv()
+        for cp in xc(b, 2):
+            start(cp)
+        start(dc(b, 2, 0))
+
+    def ex(b, *ks):
+        for k in ks:
+            for cp in xc(b, k):
+                cp.wait_recv()
+            start(dc(b, k, 1))
+
+    def ed(b):
+        for k in range(4 if b else 3):
+            for o in (0, 1):
+                dc(b, k, o).wait_recv()
+
+    pl.semaphore_wait(barrier, NT - 1 + 7)
+    for to in close:
+        pl.semaphore_signal(hop1, inc=1, device_id=to, device_id_type=MESH)
+    copies[L_W2].wait()
+    for i in (0, 1):
+        start(zc(i))
+    for cp in y1(0):
+        start(cp)
+    for i in (2, 3):
+        start(zc(i))
 
     copies[L_EMB].wait()
     copies[L_LIST].wait()
@@ -125,134 +251,9 @@
             pay[n * 8 + b * 2] = turned[0:32]
             pay[n * 8 + b * 2 + 1] = turned[64:96]
 
-    pl.semaphore_wait(barrier, NP - 1 + NT - 1)
-
-    def exchange(src, dst, ssem, rsem):
-        def one(i, carry):
-            dz, dy = far_first(i)
-            to = peer_at(dz, dy)
-            pltpu.make_async_remote_copy(
-                src_ref=src.at[to[1]], dst_ref=dst.at[p], send_sem=ssem, recv_sem=rsem,
-                device_id=to, device_id_type=MESH,
-            ).start()
-            return carry
-
-        lax.fori_loop(0, NP - 1, one, 0)
-        dst[p] = src[p]
-
-    def exchange_wait(dst, sem):
-        part = dst.at[pl.ds(0, NP - 1)]
-        pltpu.make_async_copy(part, part, sem).wait()
-
-    def towers(src, dst, ssem, rsem):
-        for i in range(1, NT):
-            to = wrap(t + i, NT)
-            pltpu.make_async_remote_copy(
-                src_ref=src.at[pl.ds(pl.multiple_of(to * CAP, CAP), CAP)],
-                dst_ref=dst.at[pl.ds(pl.multiple_of(t * CAP, CAP), CAP)],
-                send_sem=ssem, recv_sem=rsem, device_id=(to, p), device_id_type=MESH,
-            ).start()
-        mine = pl.ds(pl.multiple_of(t * CAP, CAP), CAP)
-        dst[mine] = src[mine]
-
-    def towers_wait(dst, sem):
-        part = dst.at[pl.ds(0, SLOTS - CAP)]
-        pltpu.make_async_copy(part, part, sem).wait()
-
-    ym, yp, yq = wrap(y - 1, NY), wrap(y + 1, NY), wrap(y + 2, NY)
-    SETS = (ym, yp, yq, y)
-    near = c64 + px * 32
-    other = c64 + (1 - px) * 32
-    sent = []
-
-    def start(cp):
-        cp.start()
-        sent.append(cp)
-
-    def rcopy(src, dst, ssem, rsem, to):
-        return pltpu.make_async_remote_copy(
-            src_ref=src, dst_ref=dst, send_sem=ssem, recv_sem=rsem, device_id=to, device_id_type=MESH
-        )
-
-    def rows(slot, r0, n):
-        return W2.at[slot, y, pl.ds(pl.multiple_of(near + r0, 16), n)]
-
-    def rows_b(b, k, r0, n):
-        s0, m = BATCH[b]
-        return W2.at[pl.ds(s0, m), SETS[k], pl.ds(pl.multiple_of(r0, 16), n)]
-
-    def zc(i):
-        a, b, r0, n, d = (
-            (0, 2, 0, 32, 1), (0, 3, 0, 32, -1), (0, 4, 0, 32, 2), (0, 5, 0, 32, -2),
-            (4, 6, 0, 32, 1), (5, 7, 0, 32, -1), (4, 1, 0, 16, 2), (5, 1, 16, 16, -2),
-        )[i]
-        return rcopy(rows(a, r0, n), rows(b, r0, n), zs.at[i], zr.at[i], peer_at(d, 0))
-
-    def same(part, ssem, rsem, e, to):
-        return rcopy(part, part, ssem.at[e], rsem.at[e], to)
-
-    def y1(b):
-        return [same(rows_b(b, 3, near, 32), ys, yr, b * 4 + i, peer_at(0, d)) for i, d in enumerate((1, -1))]
-
-    def y2(b):
-        return [same(rows_b(b, i, near + 16 * i, 16), ys, yr, b * 4 + 2 + i, peer_at(0, d)) for i, d in enumerate((1, -1))]
-
-    def xc(b, k):
-        return [
-            same(rows_b(b, k, near + 16 * i, 16), xs, xr, b * 8 + k * 2 + i, (wrap(x + d, NX) * NC + c, p))
-            for i, d in enumerate((1, -1))
-        ]
-
-    def dc(b, k, o):
-        return same(rows_b(b, k, other if o else near, 32), ds, dr, b * 8 + k * 2 + o, (x * NC + 1 - c, p))
-
-    def own(b):
-        for cp in y1(b) + xc(b, 3):
-            start(cp)
-        start(dc(b, 3, 0))
-
-    def ez(b):
-        for i in ((), (0, 1), (2, 3), (4, 5), (6, 7))[b]:
-            zc(i).wait_recv()
-        if b == 2:
-            for i in (4, 5, 6, 7):
-                start(zc(i))
-        own(b)
-
-    def ey(b):
-        for cp in y1(b):
-            cp.wait_recv()
-        for cp in y2(b) + xc(b, 0) + xc(b, 1):
-            start(cp)
-        for k in (0, 1):
-            start(dc(b, k, 0))
-
-    def ey2(b):
-        for cp in y2(b):
-            cp.wait_recv()
-        for cp in xc(b, 2):
-            start(cp)
-        start(dc(b, 2, 0))
-
-    def ex(b, *ks):
-        for k in ks:
-            for cp in xc(b, k):
-                cp.wait_recv()
-            start(dc(b, k, 1))
-
-    def ed(b):
-        for k in range(4 if b else 3):
-            for o in (0, 1):
-                dc(b, k, o).wait_recv()
-
-    copies[L_W2].wait()
-    for i in (0, 1):
-        start(zc(i))
-    for cp in y1(0):
-        start(cp)
-    for i in (2, 3):
-        start(zc(i))
-    exchange(pay, arr, asend, arecv)
+    pl.semaphore_wait(hop1, 4)
+    for to in close[2:]:
+        pl.semaphore_signal(hop2, inc=1, device_id=to, device_id_type=MESH)
 
     copies[L_ITEM].wait()
     for s in range(NZ):
@@ -268,6 +269,8 @@
     ey(0)
     lax.fori_loop(PAIRS // 2, PAIRS, item_step, 0)
     ez(2)
+    pl.semaphore_wait(hop2, 2)
+    exchange(pay, arr, asend, arecv)
     ey2(0)
     ey(1)
     copies[L_COT].wait()
@@ -471,6 +474,7 @@
         vm((ROWS, H2), F32), vm((ROWS, H2), BF16), vm((ROWS, H2), BF16), vm((ROWS, H2), BF16), vm((ROWS, WIDE), F32),
         dma((21,)), dma, dma, dma, dma, dma, dma, dma, dma,
         dma((8,)), dma((8,)), dma((20,)), dma((20,)), dma((40,)), dma((40,)), dma((40,)), dma((40,)),
+        pltpu.SemaphoreType.REGULAR, pltpu.SemaphoreType.REGULAR,
     ]
     anywhere = pl.BlockSpec(memory_space=pl.ANY)
     over_out, emb_grad_t = pl.pallas_call(

time: 78.1 us -> 76.4 us (0.978)
  Pallas kernels: 73.6 us -> 71.9 us
    pallas_call x1, Pallas kernels: 73.6 us -> 71.9 us  [body(): pl.pallas_call(kernel, out_shape=(jax.ShapeDtypeStruct((ROWS, H2), BF16),...]
where the time goes in v3:
time: 76.4 us; the launch traced here: 76.2 us
  Pallas kernels  71.9 us (94%)
  local copies, waits for them, and re-layouts  3.73 us (5%)
    pallas_call x1, Pallas kernels, body(): pl.pallas_call(kernel, out_shape=(jax.ShapeDtypeStruct((ROWS, H2), BF16),...  71.9 us
    unnamed x2, local copies, waits for them, and re-layouts  3.73 us

profile of v3, /device:TPU:1, one launch (start us, length us, event | category | flops | bytes accessed | tf_op | source)
XLA Modules:
  0.0 76.2 jit_solution(13558989644184658352)
XLA Ops:
  0.6 71.9 %shard_map.131 = (bf16[384,1024]{1,0:T(8,128)(2,1)}, bf16[64,2048]{1,0:T(8,128)(2,1)}) custom-call(bf16[64,2048]{1,0:T(8,128)(2,1)} %bitcast.4, s32[1,2048]{1,0:T(1,128)} %lists.1, s32[1,64]{1,0:T(1,128)} %bitcast.6, s32[1,64]{1,0:T(1,128)} %bitcast.7, bf16[384,256]{1,0:T(8,128)(2,1)} %item.1, bf16[384,1024]{1,0:T(8,128)(2,1)} %cot.1, bf16[2048,256]{1,0:T(8,128)(2,1)} %cd.1, ...), custom_call_target="tpu_custom_call" | custom-call | tf_op jit(solution)/shard_map/pallas_call | solution.py:480
  72.5 2.1 %copy.16 = bf16[384,1024]{1,0:T(8,128)(2,1)} copy(bf16[384,1024]{1,0:T(8,128)(2,1)} %get-tuple-element.8) | data formatting | bytes 1572864
  74.6 1.7 %copy.17 = bf16[2048,64]{0,1:T(8,128)(2,1)} copy(bf16[2048,64]{0,1:T(8,128)(2,1)} %bitcast.5) | data formatting | bytes 524288

commit v4 on v3

--- a/solution.py
+++ b/solution.py
@@ -46,7 +46,7 @@
     out_hbm, eg_hbm,
     embv, listv, ownv, cntv, itemv, cotv, cdv, cuv, compv, ofv, W2, otv,
     hot, pay, arr, SR, lift, tsend, trecv, gsend, grecv, bpay, barr, egv,
-    prei, hid, slope, pre2, g3, hs, gs2, outv, sacc,
+    prei, hid, slope, pre2, g3, hs, gs2, outv, cdT, cuT, compT, gcv,
     lsem, asend, arecv, tsem, trsem, gsem, grsem, bsend, brecv,
     zs, zr, ys, yr, xs, xr, ds, dr, hop1, hop2,
 ):
@@ -302,6 +302,15 @@
     tsend[:, WIDE:] = held.astype(BF16)
     for i in (L_CD, L_CU, L_COMP):
         copies[i].wait()
+
+    def turn(j, carry):
+        at = pl.ds(pl.multiple_of(j * 256, 256), 256)
+        cdT[:, at] = cdv[at, :].T
+        cuT[at, :] = cuv[:, at].T
+        compT[:, at] = compv[at, :].T
+        return carry
+
+    lax.fori_loop(0, FEAT // 256, turn, 0)
 
     exchange_wait(arr, arecv)
 
@@ -384,18 +393,19 @@
         return carry
 
     lax.fori_loop(0, 4, mid_step, 0)
-    sacc[...] = jnp.zeros_like(sacc)
-
-    def back_step(q, carry):
-        g = (dot_t(gs2[...], pair(q)) * slope[q].astype(F32)).astype(BF16)
-        sacc[...] += dot_t(g, ofv[q, :WIDE, :])
-        return carry
-
-    lax.fori_loop(0, PAIRS, back_step, 0)
+
+    held_g, acc = None, None
+    for q in range(PAIRS):
+        d = dot_t(gs2[...], pair(q))
+        if q:
+            v = dot_t(held_g, ofv[q - 1, :WIDE, :])
+            acc = v if acc is None else acc + v
+        held_g = (d * slope[q].astype(F32)).astype(BF16)
+    acc = acc + dot_t(held_g, ofv[PAIRS - 1, :WIDE, :])
     qj = iota((SLOTS, ROWS), 1)
     sj = iota((SLOTS, ROWS), 0) * MOSTC
     gather3 = jnp.where((qj >= sj) & (qj < sj + MOSTC), 1.0, 0.0).astype(BF16)
-    gsend[...] = dot(gather3, sacc[...].astype(BF16)).astype(BF16)
+    gsend[...] = dot(gather3, acc.astype(BF16)).astype(BF16)
     towers(gsend, grecv, gsem, grsem)
 
     def out_step(n, carry):
@@ -411,21 +421,31 @@
     eye = jnp.where(iota((UDEV, UDEV), 0) == iota((UDEV, UDEV), 1), 1.0, 0.0).astype(BF16)
     undisp = dot_t(eye, disp).astype(BF16)
     session_grad = dot(undisp, grecv[...]).astype(BF16)
-    gc = dot_t(session_grad, compv[...]).astype(BF16).astype(F32)
-    gl = (gc * SR[...].astype(F32)).astype(BF16)
-    glow = dot_t(gl, cuv[...]).astype(BF16)
-    lift[...] = gc * (lift[...] + 1.0) + dot_t(glow, cdv[...])
-
-    def unlay(j, carry):
-        at = pl.ds(pl.multiple_of(j * 128, 128), 128)
-        lo = lift[0:32, at]
-        hi = lift[32:64, at]
-        bpay[2 * j] = jnp.where(lane < 64, lo, pltpu.roll(hi, 64, 1)).astype(BF16)
-        bpay[2 * j + 1] = jnp.where(lane < 64, pltpu.roll(lo, 64, 1), hi).astype(BF16)
-        return carry
-
-    lax.fori_loop(0, NP // 2, unlay, 0)
-    exchange(bpay, barr, bsend, brecv)
+    gcv[...] = dot(session_grad, compT[...]).astype(BF16).astype(F32)
+    gl = (gcv[...] * SR[...].astype(F32)).astype(BF16)
+    glow = dot(gl, cuT[...]).astype(BF16)
+
+    def back_part(i, carry):
+        k = (i + 1) // 2
+        n = wrap(z // 2 + 2 + k * (1 - 2 * (i % 2)), 4)
+        at = pl.ds(pl.multiple_of(n * 512, 512), 512)
+        rows_g = gcv[:, at] * (lift[:, at] + 1.0) + dot(glow, cdT[:, at])
+        for j in range(4):
+            lo = rows_g[0:32, j * 128:(j + 1) * 128]
+            hi = rows_g[32:64, j * 128:(j + 1) * 128]
+            bpay[n * 8 + 2 * j] = jnp.where(lane < 64, lo, pltpu.roll(hi, 64, 1)).astype(BF16)
+            bpay[n * 8 + 2 * j + 1] = jnp.where(lane < 64, pltpu.roll(lo, 64, 1), hi).astype(BF16)
+        for e in range(8):
+            to = n * 8 + (e % 2) * 4 + wrap(y + (2, 1, 3, 0)[e // 2], NY)
+
+            @pl.when(to != p)
+            def _():
+                rcopy(bpay.at[to], barr.at[p], bsend, brecv, (t, to)).start()
+
+        return carry
+
+    lax.fori_loop(0, 4, back_part, 0)
+    barr[p] = bpay[p]
     for cp in sent:
         cp.wait_send()
     exchange_wait(pay, asend)
@@ -456,6 +476,23 @@
     eg_copy.wait()
 
 
+def place(a, b, out_a, out_b, held_a, held_b, sem_in, sem_out):
+    parts = [(a, held_a, out_a, r0, 96) for r0 in range(0, ROWS, 96)]
+    parts += [(b, held_b, out_b, r0, 32) for r0 in (0, 32)]
+    first, second = [], []
+    for i, (u, h, v, r0, n) in enumerate(parts):
+        at = pl.ds(r0, n)
+        first.append(pltpu.make_async_copy(u.at[at], h.at[at], sem_in.at[i]))
+        second.append(pltpu.make_async_copy(h.at[at], v.at[at], sem_out.at[i]))
+    for cp in first:
+        cp.start()
+    for cp, then in zip(first, second):
+        cp.wait()
+        then.start()
+    for cp in second:
+        cp.wait()
+
+
 def body(
     embeddings, session_lists, owners, counts, item_feats, cotangent,
     cross_down, cross_up, compress, over_first, over_second, over_third,
@@ -471,7 +508,8 @@
         vm((SLOTS, WIDE), BF16), vm((SLOTS, WIDE), BF16), vm((NP, 32, 128), BF16), vm((NP, 32, 128), BF16),
         vm((64, LISTED), BF16),
         vm((PAIRS, ROWS, HP), F32), vm((PAIRS, ROWS, HP), BF16), vm((PAIRS, ROWS, HP), BF16), vm((ROWS, H2), F32),
-        vm((ROWS, H2), F32), vm((ROWS, H2), BF16), vm((ROWS, H2), BF16), vm((ROWS, H2), BF16), vm((ROWS, WIDE), F32),
+        vm((ROWS, H2), F32), vm((ROWS, H2), BF16), vm((ROWS, H2), BF16), vm((ROWS, H2), BF16), vm((WIDE, FEAT), BF16),
+        vm((FEAT, WIDE), BF16), vm((WIDE, FEAT), BF16), vm((UDEV, FEAT), F32),
         dma((21,)), dma, dma, dma, dma, dma, dma, dma, dma,
         dma((8,)), dma((8,)), dma((20,)), dma((20,)), dma((40,)), dma((40,)), dma((40,)), dma((40,)),
         pltpu.SemaphoreType.REGULAR, pltpu.SemaphoreType.REGULAR,
@@ -493,6 +531,17 @@
         embeddings.T, session_lists, owners.reshape(1, UDEV), counts.reshape(1, UDEV), item_feats, cotangent,
         cross_down, cross_up, compress, over_first, over_second, over_third,
     )
+    over_out, emb_grad_t = pl.pallas_call(
+        place,
+        out_shape=(
+            jax.ShapeDtypeStruct((ROWS, H2), BF16),
+            jax.ShapeDtypeStruct((64, LISTED), BF16),
+        ),
+        in_specs=[anywhere] * 2,
+        out_specs=(anywhere, anywhere),
+        scratch_shapes=[vm((ROWS, H2), BF16), vm((64, LISTED), BF16), dma((6,)), dma((6,))],
+        compiler_params=pltpu.CompilerParams(vmem_limit_bytes=60 * 2**20),
+    )(over_out, emb_grad_t)
     return over_out, emb_grad_t.T
 
 

time: 76.4 us -> 71.2 us (0.932)
  local copies, waits for them, and re-layouts: 3.73 us -> 0 us
  Pallas kernels: 71.9 us -> 70.4 us
    unnamed x2 -> x0, local copies, waits for them, and re-layouts: 3.73 us -> none
    pallas_call x1, Pallas kernels: 71.9 us -> 68.4 us  [body(): pl.pallas_call(kernel, out_shape=(jax.ShapeDtypeStruct((ROWS, H2), BF16),...]
    pallas_call x0 -> x1, Pallas kernels: none -> 2.09 us  [body(): pl.pallas_call(place, out_shape=(jax.ShapeDtypeStruct((ROWS, H2), BF16),...]
where the time goes in v4:
time: 71.2 us; the launch traced here: 71.1 us
  Pallas kernels  70.4 us (99%)
    pallas_call x1, Pallas kernels, body(): pl.pallas_call(kernel, out_shape=(jax.ShapeDtypeStruct((ROWS, H2), BF16),...  68.4 us
    pallas_call x1, Pallas kernels, body(): pl.pallas_call(place, out_shape=(jax.ShapeDtypeStruct((ROWS, H2), BF16),...  2.09 us

profile of v4, /device:TPU:1, one launch (start us, length us, event | category | flops | bytes accessed | tf_op | source)
XLA Modules:
  0.0 71.1 jit_solution(16950845981447858136)
XLA Ops:
  0.6 68.4 %shard_map.131 = (bf16[384,1024]{1,0:T(8,128)(2,1)}, bf16[64,2048]{1,0:T(8,128)(2,1)}) custom-call(bf16[64,2048]{1,0:T(8,128)(2,1)} %bitcast.4, s32[1,2048]{1,0:T(1,128)} %lists.1, s32[1,64]{1,0:T(1,128)} %bitcast.5, s32[1,64]{1,0:T(1,128)} %bitcast.6, bf16[384,256]{1,0:T(8,128)(2,1)} %item.1, bf16[384,1024]{1,0:T(8,128)(2,1)} %cot.1, bf16[2048,256]{1,0:T(8,128)(2,1)} %cd.1, ...), custom_call_target="tpu_custom_call" | custom-call | tf_op jit(solution)/shard_map/pallas_call | solution.py:518
  69.0 2.1 %shard_map.132 = (bf16[384,1024]{1,0:T(8,128)(2,1)}, bf16[64,2048]{1,0:T(8,128)(2,1)}) custom-call(bf16[384,1024]{1,0:T(8,128)(2,1)} %get-tuple-element.6.a, bf16[64,2048]{1,0:T(8,128)(2,1)} %get-tuple-element.7.b), custom_call_target="tpu_custom_call" | custom-call | tf_op jit(solution)/shard_map/pallas_call | solution.py:534

commit v5 on v4

--- a/solution.py
+++ b/solution.py
@@ -371,17 +371,18 @@
     lax.fori_loop(PAIRS // 2, PAIRS, first_step, 0)
     ex(3, 0, 1)
     ex(4, 0, 1)
-    ed(1)
-    pre2[...] = dot(hid[1], pair(1))
+    ed(0)
+    pre2[...] = dot(hid[0, :, :HZ], W2[0].reshape(HZ, H2))
     ex(3, 2)
     ex(4, 2)
+    ed(1)
+    pre2[...] += dot(hid[1], pair(1))
     ed(2)
     pre2[...] += dot(hid[2], pair(2))
     ed(3)
     pre2[...] += dot(hid[3], pair(3))
-    ed(0)
     ed(4)
-    pre2[...] += dot(hid[0], pair(0))
+    pre2[...] += dot(hid[0, :, HZ:], W2[1].reshape(HZ, H2))
 
     def mid_step(n, carry):
         at = pl.ds(pl.multiple_of(n * 256, 256), 256)

time: 71.2 us -> 71.3 us (level)
  no operation moved by 1% of the time
where the time goes in v5:
time: 71.3 us; the launch traced here: 71.1 us
  Pallas kernels  70.5 us (99%)
    pallas_call x1, Pallas kernels, body(): pl.pallas_call(kernel, out_shape=(jax.ShapeDtypeStruct((ROWS, H2), BF16),...  68.4 us
    pallas_call x1, Pallas kernels, body(): pl.pallas_call(place, out_shape=(jax.ShapeDtypeStruct((ROWS, H2), BF16),...  2.09 us

profile of v5, /device:TPU:1, one launch (start us, length us, event | category | flops | bytes accessed | tf_op | source)
XLA Modules:
  0.0 71.1 jit_solution(12410923989755184737)
XLA Ops:
  0.6 68.4 %shard_map.131 = (bf16[384,1024]{1,0:T(8,128)(2,1)}, bf16[64,2048]{1,0:T(8,128)(2,1)}) custom-call(bf16[64,2048]{1,0:T(8,128)(2,1)} %bitcast.4, s32[1,2048]{1,0:T(1,128)} %lists.1, s32[1,64]{1,0:T(1,128)} %bitcast.5, s32[1,64]{1,0:T(1,128)} %bitcast.6, bf16[384,256]{1,0:T(8,128)(2,1)} %item.1, bf16[384,1024]{1,0:T(8,128)(2,1)} %cot.1, bf16[2048,256]{1,0:T(8,128)(2,1)} %cd.1, ...), custom_call_target="tpu_custom_call" | custom-call | tf_op jit(solution)/shard_map/pallas_call | solution.py:519
  69.1 2.1 %shard_map.132 = (bf16[384,1024]{1,0:T(8,128)(2,1)}, bf16[64,2048]{1,0:T(8,128)(2,1)}) custom-call(bf16[384,1024]{1,0:T(8,128)(2,1)} %get-tuple-element.6.a, bf16[64,2048]{1,0:T(8,128)(2,1)} %get-tuple-element.7.b), custom_call_target="tpu_custom_call" | custom-call | tf_op jit(solution)/shard_map/pallas_call | solution.py:535
